TPU v7x, 32 devices: a whole 2x2x4 slice. The times are simulated.
32 devices in a mesh: row: 8 (over y, x, core), col: 4 (over z).
Axes of the slice: x: 2, y: 2, z: 4, core: 2. Of those that a mesh axis runs over, the one named last changes fastest.
Arguments:
- u_factors: bfloat16 [24, 24, 1024, 128], P('row', 'col'), may hold values from -0.109375 to 0.109375
- v_factors: bfloat16 [24, 24, 1024, 128], P('row', 'col'), may hold values from -0.1875 to 0.1875
- tile_scales: float32 [24, 24, 128], P('row', 'col'), may hold values from 0.3 to 3
- rank_class: int32 [24, 24], P('row', 'col'), may hold values from 0 to 3, as said below
- slopes: float32 [64, 24576], P(None, 'row'), may hold values from -40 to 40
Outputs:
- solution_field: float32 [64, 24576], P(None, 'col')
- residual: float32 [64, 24576], P(None, 'col')
Inputs may be any that keep to these rules, and one draw needn't show every extreme that they name: `rank_class`: class k gives a tile of rank 128 / 8 * 2**k; tiles of one device tend to share high or low classes.
All inputs are finite; a program needn't handle non-finite values.
Results may differ from a plain program's by a relative error of at most 0.017.
Values may be sent and summed in bfloat16 or wider, within the bound.
A program may use at most 64 MiB of HBM per device.

v0:
```python
import jax
import jax.numpy as jnp
from jax import lax
from jax.sharding import PartitionSpec as P

ITERS = 2
damping = 0.1
epsilon = 1e-06


def rank_weights(tile_scales, rank_class):
    max_rank = tile_scales.shape[-1]
    ranks = jnp.left_shift(jnp.int32(max_rank // 8), rank_class)
    columns = lax.broadcasted_iota(jnp.int32, tile_scales.shape, 2)
    return jnp.where(columns < ranks[:, :, None], tile_scales, jnp.zeros_like(tile_scales))


def padded_apply(source, first_factor, second_factor, weights, transpose):
    rows_here, cols_here, tile_size, max_rank = first_factor.shape
    frames = source.shape[0]
    if transpose:
        pieces = source.reshape(frames, rows_here, tile_size)
        projected = jnp.einsum(
            "fis,ijsr->fijr", pieces, first_factor, preferred_element_type=jnp.float32
        )
        scaled = (projected * weights[None]).astype(jnp.bfloat16)
        result = jnp.einsum(
            "fijr,ijmr->fjm", scaled, second_factor, preferred_element_type=jnp.float32
        )
        return result.reshape(frames, cols_here * tile_size)
    pieces = source.reshape(frames, cols_here, tile_size)
    projected = jnp.einsum(
        "fjm,ijmr->fijr", pieces, first_factor, preferred_element_type=jnp.float32
    )
    scaled = (projected * weights[None]).astype(jnp.bfloat16)
    result = jnp.einsum("fijr,ijsr->fis", scaled, second_factor, preferred_element_type=jnp.float32)
    return result.reshape(frames, rows_here * tile_size)


def apply_tiles(source, first_factor, second_factor, weights, transpose):
    return padded_apply(source, first_factor, second_factor, weights, transpose)


def per_device(u_factors, v_factors, tile_scales, rank_class, slopes):
    weights = rank_weights(tile_scales, rank_class)
    rows_here, cols_here, tile_size, max_rank = u_factors.shape
    share_width = cols_here * tile_size // lax.axis_size("row")
    offset = lax.axis_index("row") * share_width

    def backward(image_b):
        partial_value = apply_tiles(image_b, u_factors, v_factors, weights, True)
        return lax.psum(partial_value, "row")

    def own_part(field):
        return lax.dynamic_slice_in_dim(field, offset, share_width, 1)

    def frame_product(left_field, right_field):
        return jnp.sum(own_part(left_field) * own_part(right_field), axis=1)

    right_side = backward(slopes.astype(jnp.bfloat16))
    solution_field = jnp.zeros_like(right_side)
    residual = right_side
    direction = right_side
    norm_now = lax.psum(frame_product(residual, residual), ("row", "col"))
    dir_norm = norm_now
    for sweep in range(ITERS):
        narrowed = direction.astype(jnp.bfloat16)
        forward_partial_value = apply_tiles(narrowed, v_factors, u_factors, weights, False)
        forward_image = lax.psum(forward_partial_value, "col")
        image_norm = lax.psum(jnp.sum(forward_image * forward_image, axis=1), "row")
        dir_norm = lax.psum(frame_product(direction, direction), ("row", "col"))
        operator_image = backward(forward_image.astype(jnp.bfloat16)) + damping * direction
        step_size = norm_now / (image_norm + damping * dir_norm + epsilon)
        solution_field = solution_field + step_size[:, None] * direction
        residual = residual - step_size[:, None] * operator_image
        if sweep + 1 < ITERS:
            norm_next = lax.psum(frame_product(residual, residual), ("row", "col"))
            growth = norm_next / (norm_now + epsilon)
            direction = residual + growth[:, None] * direction
            norm_now = norm_next
    return (solution_field, residual)


def solution(mesh):
    return jax.shard_map(
        per_device,
        mesh=mesh,
        in_specs=(
            P("row", "col", None, None),
            P("row", "col", None, None),
            P("row", "col", None),
            P("row", "col"),
            P(None, "row"),
        ),
        out_specs=(P(None, "col"), P(None, "col")),
        check_vma=False,
    )
```

profile of v0, /device:TPU:0, one launch (start us, length us, event | category | flops | bytes accessed | tf_op | source)
XLA Modules:
  0.0 383.3 jit_solution(15641545947727971645)
XLA Ops:
  8.7 1.2 convert_element_type.39
  10.4 6.1 %fusion.12 = f32[6,8,8,1024]{3,2,1,0:T(8,128)S(1)} fusion(bf16[3,6,1024,128]{3,2,1,0:T(8,128)(2,1)} %param.6, bf16[3,6,1024,128]{3,2,1,0:T(8,128)(2,1)} %param.5, bf16[64,3,1024,1]{2,1,0,3:T(4,128)(2,1)S(1)} %reshape.49, f32[3,6,128]{2,0,1:T(4,128)S(1)} %copy.12), kind=kOutput, calls=%fused_computation.16 | convolution fusion | flops 604274688 | bytes 11412480 | tf_op jit(solution)/shard_map/fijr,ijmr->fjm/dot_general | solution.py:27
  16.5 1.3 copy.33
  17.9 61.8 %all-reduce.6.cloned.1.call-done = f32[64,6144]{1,0:T(8,128)} async-done(((f32[64,6144]{1,0:T(8,128)}), f32[64,6144]{1,0:T(8,128)}) %all-reduce.6.cloned.1.call-update) | async-done | bytes 1572880 | tf_op jit(solution)/shard_map/psum | solution.py:52
  79.7 1.5 convert_element_type.42
  81.2 1.0 reshape.51
  82.2 6.6 %convolution_bitcast_fusion.1 = f32[3,8,8,1024]{3,2,1,0:T(8,128)S(1)} fusion(bf16[3,6,1024,128]{3,2,1,0:T(8,128)(2,1)} %param.5, bf16[3,6,1024,128]{3,2,1,0:T(8,128)(2,1)} %param.6, bf16[64,6,1024,1]{2,1,0,3:T(8,128)(2,1)S(1)} %reshape.51, f32[3,6,128]{2,1,0:T(8,128)S(1)} %fusion.73), kind=kOutput, calls=%fused_computation.20 | convolution fusion | flops 604274688 | bytes 11019264 | tf_op jit(solution)/shard_map/fijr,ijsr->fis/dot_general | solution.py:36
  88.7 0.9 copy.34
  89.7 43.1 %all-reduce.8.cloned.1.call-done = f32[64,3072]{1,0:T(8,128)} async-done(((f32[64,3072]{1,0:T(8,128)}), f32[64,3072]{1,0:T(8,128)}) %all-reduce.8.cloned.1.call-update) | async-done | bytes 786448 | tf_op jit(solution)/shard_map/psum | solution.py:69
  132.9 1.6 multiply_reduce_fusion.1
  135.0 6.1 %fusion.15 = f32[6,8,8,1024]{3,2,1,0:T(8,128)S(1)} fusion(bf16[3,6,1024,128]{3,2,1,0:T(8,128)(2,1)} %param.6, bf16[3,6,1024,128]{3,2,1,0:T(8,128)(2,1)} %param.5, bf16[64,3,1024,1]{2,1,0,3:T(4,128)(2,1)S(1)} %reshape.53, f32[3,6,128]{2,0,1:T(4,128)S(1)} %copy.12), kind=kOutput, calls=%fused_computation.17 | convolution fusion | flops 604274688 | bytes 11412480 | tf_op jit(solution)/shard_map/fijr,ijmr->fjm/dot_general | solution.py:27
  141.1 1.3 copy.35
  142.5 1.3 copy-done
  143.9 39.8 %psum.74 = f32[64]{0:T(128)S(1)} all-reduce(f32[64]{0:T(128)S(1)} %multiply_reduce_fusion.4), channel_id=1, replica_groups=mesh['row'=8,'col'=4] {'row','col'}, use_global_device_ids=true, to_apply=%region_2.3 | all-reduce | flops 64 | bytes 512 | tf_op jit(solution)/shard_map/psum | solution.py:64
  183.8 12.9 %psum.76 = f32[64]{0:T(128)S(1)} all-reduce(f32[64]{0:T(128)S(1)} %get-tuple-element.8), channel_id=1, replica_groups=mesh['row'=8,'col'=4] {'row'}, use_global_device_ids=true, to_apply=%region_5.6 | all-reduce | flops 64 | bytes 512 | tf_op jit(solution)/shard_map/psum | solution.py:70
  196.7 4.7 %all-reduce.10.cloned.1.call-done = f32[64,6144]{1,0:T(8,128)} async-done(((f32[64,6144]{1,0:T(8,128)}), f32[64,6144]{1,0:T(8,128)}) %all-reduce.10.cloned.1.call-update) | async-done | bytes 1572880 | tf_op jit(solution)/shard_map/psum | solution.py:52
  201.4 1.7 multiply_subtract_fusion.1
  203.2 39.7 %psum.78 = f32[64]{0:T(128)S(1)} all-reduce(f32[64]{0:T(128)S(1)} %multiply_reduce_fusion.3), channel_id=1, replica_groups=mesh['row'=8,'col'=4] {'row','col'}, use_global_device_ids=true, to_apply=%region_8.9 | all-reduce | flops 64 | bytes 512 | tf_op jit(solution)/shard_map/psum | solution.py:77
  242.8 1.7 fusion.74
  244.5 2.8 reshape.55
  247.3 7.7 %convolution_bitcast_fusion = f32[3,8,8,1024]{3,2,1,0:T(8,128)} fusion(bf16[3,6,1024,128]{3,2,1,0:T(8,128)(2,1)} %param.5, bf16[3,6,1024,128]{3,2,1,0:T(8,128)(2,1)} %param.6, bf16[64,6,1024,1]{2,1,0,3:T(8,128)(2,1)} %reshape.55, f32[3,6,128]{2,1,0:T(8,128)S(1)} %fusion.73), kind=kOutput, calls=%fused_computation.19 | convolution fusion | flops 604274688 | bytes 11019264 | tf_op jit(solution)/shard_map/fijr,ijsr->fis/dot_general | solution.py:36
  255.1 2.1 copy.36
  257.2 43.6 %all-reduce.12.cloned.1.call-done = f32[64,3072]{1,0:T(8,128)} async-done(((f32[64,3072]{1,0:T(8,128)}), f32[64,3072]{1,0:T(8,128)}) %all-reduce.12.cloned.1.call-update) | async-done | bytes 786448 | tf_op jit(solution)/shard_map/psum | solution.py:69
  300.8 2.1 fusion.75
  302.9 1.3 reshape.57
  304.1 7.4 %fusion.18 = f32[6,8,8,1024]{3,2,1,0:T(8,128)} fusion(bf16[3,6,1024,128]{3,2,1,0:T(8,128)(2,1)} %param.6, bf16[3,6,1024,128]{3,2,1,0:T(8,128)(2,1)} %param.5, bf16[64,3,1024,1]{2,1,0,3:T(4,128)(2,1)} %reshape.57, f32[3,6,128]{2,0,1:T(4,128)S(1)} %copy.12), kind=kOutput, calls=%fused_computation.18 | convolution fusion | flops 604274688 | bytes 11412480 | tf_op jit(solution)/shard_map/fijr,ijmr->fjm/dot_general | solution.py:27
  311.5 2.7 copy.37
  314.3 1.0 multiply_reduce_fusion.2
  315.3 40.0 %psum.81 = f32[64]{0:T(128)S(1)} all-reduce(f32[64]{0:T(128)S(1)} %multiply_reduce_fusion.2), channel_id=1, replica_groups=mesh['row'=8,'col'=4] {'row','col'}, use_global_device_ids=true, to_apply=%region_13.14 | all-reduce | flops 64 | bytes 512 | tf_op jit(solution)/shard_map/psum | solution.py:71
  355.3 12.9 %psum.80 = f32[64]{0:T(128)S(1)} all-reduce(f32[64]{0:T(128)S(1)} %copy-done.1), channel_id=1, replica_groups=mesh['row'=8,'col'=4] {'row'}, use_global_device_ids=true, to_apply=%region_11.12 | all-reduce | flops 64 | bytes 512 | tf_op jit(solution)/shard_map/psum | solution.py:70
  368.2 4.6 %all-reduce.14.cloned.1.call-done = f32[64,6144]{1,0:T(8,128)} async-done(((f32[64,6144]{1,0:T(8,128)}), f32[64,6144]{1,0:T(8,128)}) %all-reduce.14.cloned.1.call-update) | async-done | bytes 1572880 | tf_op jit(solution)/shard_map/psum | solution.py:52
  372.8 4.0 %multiply_subtract_fusion = (f32[64,6144]{1,0:T(8,128)}, f32[64,6144]{1,0:T(8,128)}) fusion(f32[64,6144]{1,0:T(8,128)S(1)} %multiply_subtract_fusion.1, f32[64,6144]{1,0:T(8,128)} %all-reduce.14.cloned.1.call-done, f32[64,6144]{1,0:T(8,128)} %get-tuple-element.3, f32[64]{0:T(128)S(1)} %add_divide_fusion, f32[64,6144]{1,0:T(8,128)S(1)} %copy-done, ...), kind=kLoop, calls=%fused_computation.12 | loop fusion | flops 2752512 | bytes 9437696 | tf_op jit(solution)/shard_map/sub | solution.py:75
  (27 shorter events, 3.2 us)
Async XLA Ops:
  7.2 72.5 %all-reduce.6.cloned.1.call-start = ((), (), s32[]{:S(2)}) async-start(), calls=%async_computation | async-start | bytes 3145728 | tf_op jit(solution)/shard_map/psum | solution.py:52
  17.9 115.0 %all-reduce.8.cloned.1.call-start = ((), (), s32[]{:S(2)}) async-start(), calls=%async_computation.1 | async-start | bytes 1572864 | tf_op jit(solution)/shard_map/psum | solution.py:69
  89.7 111.7 %all-reduce.10.cloned.1.call-start = ((), (), s32[]{:S(2)}) async-start(), calls=%async_computation.2 | async-start | bytes 3145728 | tf_op jit(solution)/shard_map/psum | solution.py:52
  142.4 1.4 copy-start
  142.4 158.4 %all-reduce.12.cloned.1.call-start = ((), (), s32[]{:S(2)}) async-start(), calls=%async_computation.3 | async-start | bytes 1572864 | tf_op jit(solution)/shard_map/psum | solution.py:69
  242.8 1.7 copy-start.2
  257.2 115.6 %all-reduce.14.cloned.1.call-start = ((), (), s32[]{:S(2)}) async-start(), calls=%async_computation.4 | async-start | bytes 3145728 | tf_op jit(solution)/shard_map/psum | solution.py:52
  314.2 41.0 %copy-start.1 = (f32[64]{0:T(128)S(1)}, f32[64]{0:T(128)}, u32[]{:S(2)}) copy-start(f32[64]{0:T(128)} %get-tuple-element.7) | copy-start | bytes 772
  314.2 54.0 %copy-start.3 = (f32[64]{0:T(128)S(1)}, f32[64]{0:T(128)}, u32[]{:S(2)}) copy-start(f32[64]{0:T(128)} %copy-done.2) | copy-start | bytes 772
Sparse Core Ops, SparseCore 0:
  18.0 61.6 all-reduce.5
  89.8 43.0 all-reduce.7
  142.6 58.7 all-reduce.9
  257.3 43.4 all-reduce.11
  314.4 58.3 all-reduce.13
where the time goes:
time: 384 us; the launch traced here: 383 us
  waiting for transfers between devices  158 us (41%)
  blocking collectives  145 us (38%)
  matrix products  33.8 us (9%)
  other arithmetic  16.4 us (4%)
  local copies, waits for them, and re-layouts  15.9 us (4%)
  between operations  13.9 us (4%)
    psum x2, waiting for transfers between devices, per_device(): forward_image = lax.psum(forward_partial_value, 'col')  86.7 us
    psum x3, waiting for transfers between devices, backward(): return lax.psum(partial_value, 'row')  71 us
    psum x1, blocking collectives, per_device(): dir_norm = lax.psum(frame_product(direction, direction), ('row', 'col'))  40 us
    psum x1, blocking collectives, per_device(): norm_now = lax.psum(frame_product(residual, residual), ('row', 'col'))  39.8 us
    psum x1, blocking collectives, per_device(): norm_next = lax.psum(frame_product(residual, residual), ('row', 'col'))  39.7 us
    psum x2, blocking collectives, per_device(): image_norm = lax.psum(jnp.sum(forward_image * forward_image, axis=1), 'row')  25.8 us
    dot_general x3, matrix products, padded_apply(): jnp.einsum('fijr,ijmr->fjm', scaled, second_factor, preferred_element_typ...  19.5 us
    dot_general x2, matrix products, padded_apply(): jnp.einsum('fijr,ijsr->fis', scaled, second_factor, preferred_element_typ...  14.3 us
  transfers between devices with their start and end apart: 5, of which 5 were waited for; matrix products, arithmetic and copies ran while one was open for 0% of the time, Pallas kernels for 0%

commit v1 on v0

--- a/solution.py
+++ b/solution.py
@@ -66,7 +66,10 @@
     for sweep in range(ITERS):
         narrowed = direction.astype(jnp.bfloat16)
         forward_partial_value = apply_tiles(narrowed, v_factors, u_factors, weights, False)
-        forward_image = lax.psum(forward_partial_value, "col")
+        devices, forward_image = (lax.axis_size("col"), forward_partial_value)
+        for hop in [1 << k for k in range(devices.bit_length() - 1)]:
+            swap = [(i, i ^ hop) for i in range(devices)]
+            forward_image = forward_image + lax.ppermute(forward_image, "col", swap)
         image_norm = lax.psum(jnp.sum(forward_image * forward_image, axis=1), "row")
         dir_norm = lax.psum(frame_product(direction, direction), ("row", "col"))
         operator_image = backward(forward_image.astype(jnp.bfloat16)) + damping * direction

time: 384 us -> 401 us (1.044)
  waiting for transfers between devices: 158 us -> 174 us
  starting transfers between devices: 0.21 us -> 8.26 us
    ppermute x0 -> x4, waiting for transfers between devices: none -> 99.3 us  [per_device(): forward_image = forward_image + lax.ppermute(forward_image, 'col', swap)]
    psum x2 -> x0, waiting for transfers between devices: 86.7 us -> none  [per_device(): forward_image = lax.psum(forward_partial_value, 'col')]
    ppermute x0 -> x4, starting transfers between devices: none -> 8.14 us  [per_device(): forward_image = forward_image + lax.ppermute(forward_image, 'col', swap)]
  transfers between devices with their start and end apart: 5 -> 7, of which waited for: 5 -> 7; matrix products, arithmetic and copies ran while one was open for 0% -> 0% of each run, Pallas kernels for 0% -> 0%
where the time goes in v1:
time: 401 us; the launch traced here: 400 us
  waiting for transfers between devices  174 us (43%)
  blocking collectives  142 us (35%)
  matrix products  33.8 us (8%)
  local copies, waits for them, and re-layouts  14.2 us (4%)
  other arithmetic  13.9 us (3%)
  between operations  13.8 us (3%)
  starting transfers between devices  8.26 us (2%)
    ppermute x4, waiting for transfers between devices, per_device(): forward_image = forward_image + lax.ppermute(forward_image, 'col', swap)  99.3 us
    psum x3, waiting for transfers between devices, backward(): return lax.psum(partial_value, 'row')  74.6 us
    psum x1, blocking collectives, per_device(): norm_next = lax.psum(frame_product(residual, residual), ('row', 'col'))  39.7 us
    psum x1, blocking collectives, per_device(): norm_now = lax.psum(frame_product(residual, residual), ('row', 'col'))  38.6 us
    psum x1, blocking collectives, per_device(): dir_norm = lax.psum(frame_product(direction, direction), ('row', 'col'))  38.4 us
    psum x2, blocking collectives, per_device(): image_norm = lax.psum(jnp.sum(forward_image * forward_image, axis=1), 'row')  25.6 us
    dot_general x3, matrix products, padded_apply(): jnp.einsum('fijr,ijmr->fjm', scaled, second_factor, preferred_element_typ...  19.6 us
    dot_general x2, matrix products, padded_apply(): jnp.einsum('fijr,ijsr->fis', scaled, second_factor, preferred_element_typ...  14.3 us
  transfers between devices with their start and end apart: 7, of which 7 were waited for; matrix products, arithmetic and copies ran while one was open for 0% of the time, Pallas kernels for 0%

profile of v1, /device:TPU:0, one launch (start us, length us, event | category | flops | bytes accessed | tf_op | source)
XLA Modules:
  0.0 400.2 jit_solution(4874403974233068478)
XLA Ops:
  10.4 6.1 %fusion.12 = f32[6,8,8,1024]{3,2,1,0:T(8,128)S(1)} fusion(bf16[3,6,1024,128]{3,2,1,0:T(8,128)(2,1)} %param.6, bf16[3,6,1024,128]{3,2,1,0:T(8,128)(2,1)} %param.5, bf16[64,3,1024,1]{2,1,0,3:T(4,128)(2,1)S(1)} %reshape.49, f32[3,6,128]{2,0,1:T(4,128)S(1)} %copy.12), kind=kOutput, calls=%fused_computation.16 | convolution fusion | flops 604274688 | bytes 11412480 | tf_op jit(solution)/shard_map/fijr,ijmr->fjm/dot_general | solution.py:27
  16.5 1.3 copy.33
  17.9 61.8 %all-reduce.4.cloned.1.call-done = f32[64,6144]{1,0:T(8,128)} async-done(((f32[64,6144]{1,0:T(8,128)}), f32[64,6144]{1,0:T(8,128)}) %all-reduce.4.cloned.1.call-update) | async-done | bytes 1572880 | tf_op jit(solution)/shard_map/psum | solution.py:52
  79.7 1.5 convert_element_type.42
  82.2 6.6 %convolution_bitcast_fusion.1 = f32[3,8,8,1024]{3,2,1,0:T(8,128)S(1)} fusion(bf16[3,6,1024,128]{3,2,1,0:T(8,128)(2,1)} %param.5, bf16[3,6,1024,128]{3,2,1,0:T(8,128)(2,1)} %param.6, bf16[64,6,1024,1]{2,1,0,3:T(8,128)(2,1)S(1)} %reshape.51, f32[3,6,128]{2,1,0:T(8,128)S(1)} %fusion.73), kind=kOutput, calls=%fused_computation.20 | convolution fusion | flops 604274688 | bytes 11019264 | tf_op jit(solution)/shard_map/fijr,ijsr->fis/dot_general | solution.py:36
  88.8 1.7 collective-permute-start
  90.5 16.7 %collective-permute-done = f32[64,3072]{1,0:T(8,128)S(1)} collective-permute-done((f32[64,3072]{1,0:T(8,128)S(1)}, f32[64,3072]{1,0:T(8,128)S(1)}, u32[]{:S(2)}, u32[]{:S(2)}) %collective-permute-start) | collective-permute-done | bytes 786464 | tf_op jit(solution)/shard_map/ppermute | solution.py:72
  107.2 2.5 collective-permute-start.1
  109.7 32.7 %collective-permute-done.1 = f32[64,3072]{1,0:T(8,128)S(1)} collective-permute-done((f32[64,3072]{1,0:T(8,128)S(1)}, f32[64,3072]{1,0:T(8,128)S(1)}, u32[]{:S(2)}, u32[]{:S(2)}) %collective-permute-start.1) | collective-permute-done | bytes 786464 | tf_op jit(solution)/shard_map/ppermute | solution.py:72
  143.2 6.1 %fusion.15 = f32[6,8,8,1024]{3,2,1,0:T(8,128)S(1)} fusion(bf16[3,6,1024,128]{3,2,1,0:T(8,128)(2,1)} %param.6, bf16[3,6,1024,128]{3,2,1,0:T(8,128)(2,1)} %param.5, bf16[64,3,1024,1]{2,1,0,3:T(4,128)(2,1)S(1)} %reshape.53, f32[3,6,128]{2,0,1:T(4,128)S(1)} %copy.12), kind=kOutput, calls=%fused_computation.17 | convolution fusion | flops 604274688 | bytes 11412480 | tf_op jit(solution)/shard_map/fijr,ijmr->fjm/dot_general | solution.py:27
  149.3 1.3 copy.35
  150.7 1.3 copy-done
  152.1 38.6 %psum.60 = f32[64]{0:T(128)S(1)} all-reduce(f32[64]{0:T(128)S(1)} %multiply_reduce_fusion.4), channel_id=1, replica_groups=mesh['row'=8,'col'=4] {'row','col'}, use_global_device_ids=true, to_apply=%region_2.3 | all-reduce | flops 64 | bytes 512 | tf_op jit(solution)/shard_map/psum | solution.py:64
  190.7 12.8 %psum.61 = f32[64]{0:T(128)S(1)} all-reduce(f32[64]{0:T(128)S(1)} %get-tuple-element.8), channel_id=1, replica_groups=mesh['row'=8,'col'=4] {'row'}, use_global_device_ids=true, to_apply=%region_4.5 | all-reduce | flops 64 | bytes 512 | tf_op jit(solution)/shard_map/psum | solution.py:73
  203.5 6.2 %all-reduce.6.cloned.1.call-done = f32[64,6144]{1,0:T(8,128)} async-done(((f32[64,6144]{1,0:T(8,128)}), f32[64,6144]{1,0:T(8,128)}) %all-reduce.6.cloned.1.call-update) | async-done | bytes 1572880 | tf_op jit(solution)/shard_map/psum | solution.py:52
  209.7 1.7 multiply_subtract_fusion.1
  211.5 39.7 %psum.63 = f32[64]{0:T(128)S(1)} all-reduce(f32[64]{0:T(128)S(1)} %multiply_reduce_fusion.3), channel_id=1, replica_groups=mesh['row'=8,'col'=4] {'row','col'}, use_global_device_ids=true, to_apply=%region_7.8 | all-reduce | flops 64 | bytes 512 | tf_op jit(solution)/shard_map/psum | solution.py:80
  251.2 1.7 fusion.74
  252.9 2.8 reshape.55
  255.7 7.7 %convolution_bitcast_fusion = f32[3,8,8,1024]{3,2,1,0:T(8,128)} fusion(bf16[3,6,1024,128]{3,2,1,0:T(8,128)(2,1)} %param.5, bf16[3,6,1024,128]{3,2,1,0:T(8,128)(2,1)} %param.6, bf16[64,6,1024,1]{2,1,0,3:T(8,128)(2,1)} %reshape.55, f32[3,6,128]{2,1,0:T(8,128)S(1)} %fusion.73), kind=kOutput, calls=%fused_computation.19 | convolution fusion | flops 604274688 | bytes 11019264 | tf_op jit(solution)/shard_map/fijr,ijsr->fis/dot_general | solution.py:36
  263.5 1.2 copy.36
  264.7 1.6 collective-permute-start.2
  266.2 17.0 %collective-permute-done.2 = f32[64,3072]{1,0:T(8,128)S(1)} collective-permute-done((f32[64,3072]{1,0:T(8,128)S(1)}, f32[64,3072]{1,0:T(8,128)S(1)}, u32[]{:S(2)}, u32[]{:S(2)}) %collective-permute-start.2) | collective-permute-done | bytes 786464 | tf_op jit(solution)/shard_map/ppermute | solution.py:72
  283.3 2.4 collective-permute-start.3
  285.7 33.0 %collective-permute-done.3 = f32[64,3072]{1,0:T(8,128)S(1)} collective-permute-done((f32[64,3072]{1,0:T(8,128)S(1)}, f32[64,3072]{1,0:T(8,128)S(1)}, u32[]{:S(2)}, u32[]{:S(2)}) %collective-permute-start.3) | collective-permute-done | bytes 786464 | tf_op jit(solution)/shard_map/ppermute | solution.py:72
  319.4 1.3 reshape.57
  320.6 7.4 %fusion.18 = f32[6,8,8,1024]{3,2,1,0:T(8,128)} fusion(bf16[3,6,1024,128]{3,2,1,0:T(8,128)(2,1)} %param.6, bf16[3,6,1024,128]{3,2,1,0:T(8,128)(2,1)} %param.5, bf16[64,3,1024,1]{2,1,0,3:T(4,128)(2,1)} %reshape.57, f32[3,6,128]{2,0,1:T(4,128)S(1)} %copy.12), kind=kOutput, calls=%fused_computation.18 | convolution fusion | flops 604274688 | bytes 11412480 | tf_op jit(solution)/shard_map/fijr,ijmr->fjm/dot_general | solution.py:27
  328.0 2.7 copy.37
  331.8 38.4 %psum.65 = f32[64]{0:T(128)S(1)} all-reduce(f32[64]{0:T(128)S(1)} %multiply_reduce_fusion.2), channel_id=1, replica_groups=mesh['row'=8,'col'=4] {'row','col'}, use_global_device_ids=true, to_apply=%region_11.12 | all-reduce | flops 64 | bytes 512 | tf_op jit(solution)/shard_map/psum | solution.py:74
  370.2 12.8 %psum.64 = f32[64]{0:T(128)S(1)} all-reduce(f32[64]{0:T(128)S(1)} %copy-done.1), channel_id=1, replica_groups=mesh['row'=8,'col'=4] {'row'}, use_global_device_ids=true, to_apply=%region_9.10 | all-reduce | flops 64 | bytes 512 | tf_op jit(solution)/shard_map/psum | solution.py:73
  383.0 6.6 %all-reduce.8.cloned.1.call-done = f32[64,6144]{1,0:T(8,128)} async-done(((f32[64,6144]{1,0:T(8,128)}), f32[64,6144]{1,0:T(8,128)}) %all-reduce.8.cloned.1.call-update) | async-done | bytes 1572880 | tf_op jit(solution)/shard_map/psum | solution.py:52
  389.7 4.0 %multiply_subtract_fusion = (f32[64,6144]{1,0:T(8,128)}, f32[64,6144]{1,0:T(8,128)}) fusion(f32[64,6144]{1,0:T(8,128)S(1)} %multiply_subtract_fusion.1, f32[64,6144]{1,0:T(8,128)} %all-reduce.8.cloned.1.call-done, f32[64,6144]{1,0:T(8,128)} %get-tuple-element.3, f32[64]{0:T(128)S(1)} %add_divide_fusion, f32[64,6144]{1,0:T(8,128)S(1)} %copy-done, ...), kind=kLoop, calls=%fused_computation.12 | loop fusion | flops 2752512 | bytes 9437696 | tf_op jit(solution)/shard_map/sub | solution.py:78
  (31 shorter events, 7.4 us)
Async XLA Ops:
  7.2 72.5 %all-reduce.4.cloned.1.call-start = ((), (), s32[]{:S(2)}) async-start(), calls=%async_computation | async-start | bytes 3145728 | tf_op jit(solution)/shard_map/psum | solution.py:52
  17.9 191.8 %all-reduce.6.cloned.1.call-start = ((), (), s32[]{:S(2)}) async-start(), calls=%async_computation.1 | async-start | bytes 3145728 | tf_op jit(solution)/shard_map/psum | solution.py:52
  88.8 18.4 %collective-permute-start = (f32[64,3072]{1,0:T(8,128)S(1)}, f32[64,3072]{1,0:T(8,128)S(1)}, u32[]{:S(2)}, u32[]{:S(2)}) collective-permute-start(f32[64,3072]{1,0:T(8,128)S(1)} %bitcast.70), channel_id=1, source_target_pairs={{0,1},{1,0},{2,3},{3,2},{4,5},{5,4},{6,7},{7,6},{8,9},{9,8},{10,11... | collective-permute-start | bytes 2359304 | tf_op jit(solution)/shard_map/ppermute | solution.py:72
  107.2 35.2 %collective-permute-start.1 = (f32[64,3072]{1,0:T(8,128)S(1)}, f32[64,3072]{1,0:T(8,128)S(1)}, u32[]{:S(2)}, u32[]{:S(2)}) collective-permute-start(f32[64,3072]{1,0:T(8,128)S(1)} %add.67), channel_id=1, source_target_pairs={{0,2},{1,3},{2,0},{3,1},{4,6},{5,7},{6,4},{7,5},{8,10},{9,11},{10,... | collective-permute-start | bytes 2359304 | tf_op jit(solution)/shard_map/ppermute | solution.py:72
  150.6 1.4 copy-start
  150.6 239.1 %all-reduce.8.cloned.1.call-start = ((), (), s32[]{:S(2)}) async-start(), calls=%async_computation.2 | async-start | bytes 3145728 | tf_op jit(solution)/shard_map/psum | solution.py:52
  251.2 1.7 copy-start.2
  264.7 18.5 %collective-permute-start.2 = (f32[64,3072]{1,0:T(8,128)S(1)}, f32[64,3072]{1,0:T(8,128)S(1)}, u32[]{:S(2)}, u32[]{:S(2)}) collective-permute-start(f32[64,3072]{1,0:T(8,128)S(1)} %bitcast.72), channel_id=1, source_target_pairs={{0,1},{1,0},{2,3},{3,2},{4,5},{5,4},{6,7},{7,6},{8,9},{9,8},{10,11... | collective-permute-start | bytes 2359304 | tf_op jit(solution)/shard_map/ppermute | solution.py:72
  283.3 35.4 %collective-permute-start.3 = (f32[64,3072]{1,0:T(8,128)S(1)}, f32[64,3072]{1,0:T(8,128)S(1)}, u32[]{:S(2)}, u32[]{:S(2)}) collective-permute-start(f32[64,3072]{1,0:T(8,128)S(1)} %add.74), channel_id=1, source_target_pairs={{0,2},{1,3},{2,0},{3,1},{4,6},{5,7},{6,4},{7,5},{8,10},{9,11},{10,... | collective-permute-start | bytes 2359304 | tf_op jit(solution)/shard_map/ppermute | solution.py:72
  330.7 39.5 %copy-start.1 = (f32[64]{0:T(128)S(1)}, f32[64]{0:T(128)}, u32[]{:S(2)}) copy-start(f32[64]{0:T(128)} %get-tuple-element.7) | copy-start | bytes 772
  330.7 52.3 %copy-start.3 = (f32[64]{0:T(128)S(1)}, f32[64]{0:T(128)}, u32[]{:S(2)}) copy-start(f32[64]{0:T(128)} %copy-done.2) | copy-start | bytes 772
Sparse Core Ops, SparseCore 0:
  18.0 61.6 all-reduce.3
  150.7 58.9 all-reduce.5
  330.9 58.7 all-reduce.7
